TPU v7x, 32 devices: a whole 2x2x4 slice. The times are simulated.
32 devices in a mesh: exp: 16 (over z, x, core), tp: 2 (over y).
Axes of the slice: x: 2, y: 2, z: 4, core: 2. Of those that a mesh axis runs over, the one named last changes fastest.
Arguments:
- tokens: bfloat16 [8192, 1024], P(('exp', 'tp')), may hold values from -6 to 6
- gain_attn: float32 [1024], replicated, may hold values from 0.1 to 1.9
- w_query: bfloat16 [1024, 1024], P(None, 'tp'), may hold values from -0.25 to 0.25
- w_key: bfloat16 [1024, 512], P(None, 'tp'), may hold values from -0.25 to 0.25
- w_value: bfloat16 [1024, 512], P(None, 'tp'), may hold values from -0.1875 to 0.1875
- w_out: bfloat16 [1024, 1024], replicated, may hold values from -0.5 to 0.5
- gain_ffn: float32 [1024], replicated, may hold values from 0.1 to 1.9
- w_router: bfloat16 [1024, 32], replicated, may hold values from -0.09375 to 0.09375
- w_gate: bfloat16 [32, 1024, 512], P('exp', None, 'tp'), may hold values from -0.1875 to 0.1875
- w_up: bfloat16 [32, 1024, 512], P('exp', None, 'tp'), may hold values from -0.1875 to 0.1875
- w_down: bfloat16 [32, 512, 1024], P('exp', 'tp'), may hold values from -1 to 1
- segment_ids: int32 [8192], P('exp'), may hold values from 0 to 15, never falling along the last dimension, each value on 1 to 2000 neighbouring positions
- routes: int32 [8192, 8], P(('exp', 'tp')), may hold values from 0 to 31, all different within a row; in each aligned block of 256 rows (0 to 255, 256 to 511, ...) at most 128 rows name the same one
- out_grad: bfloat16 [8192, 1024], P(('exp', 'tp')), may hold values from -6 to 6
Outputs:
- output: bfloat16 [8192, 1024], P(('exp', 'tp'))
- input_grad: float32 [8192, 1024], P(('exp', 'tp'))
- gain_attn_grad: float32 [1024], replicated
- w_query_grad: float32 [1024, 1024], P(None, 'tp')
- w_key_grad: float32 [1024, 512], P(None, 'tp')
- w_value_grad: float32 [1024, 512], P(None, 'tp')
- w_out_grad: float32 [1024, 1024], replicated
- gain_ffn_grad: float32 [1024], replicated
- w_router_grad: float32 [1024, 32], replicated
- w_gate_grad: float32 [32, 1024, 512], P('exp', None, 'tp')
- w_up_grad: float32 [32, 1024, 512], P('exp', None, 'tp')
- w_down_grad: float32 [32, 512, 1024], P('exp', 'tp')
Inputs may be any that keep to these rules, and one draw needn't show every extreme that they name: `routes`: each row names 8 different experts. In the rows of one device (aligned blocks of 256 rows) each expert is named by at most 128 rows, a bound that some block reaches. `segment_ids`: never falling along the array; each document number covers 1 to 2000 consecutive tokens, one exactly 2000.
All inputs are finite; a program needn't handle non-finite values.
Results may differ from a plain program's by a relative error of at most 0.023.
Values may be sent and summed in bfloat16 or wider, within the bound.
A program may use at most 192 MiB of HBM per device.

v0:
```python
import jax
import jax.numpy as jnp
from jax import lax
from jax.sharding import PartitionSpec as P

HEAD = 64
SEQ_LEN = 512
CAP = 128
epsilon = 1e-06
base_theta = 10000.0


def contract(left, right, left_dim, right_dim):
    return lax.dot_general(
        left, right, (((left_dim,), (right_dim,)), ((), ())), preferred_element_type=jnp.float32
    )


def doc_positions(seg_rows):
    indices = jnp.arange(seg_rows.shape[-1], dtype=jnp.int32)
    previous = jnp.concatenate([seg_rows[..., :1], seg_rows[..., :-1]], axis=-1)
    starts = (indices == 0) | (seg_rows != previous)
    latest = lax.cummax(jnp.where(starts, indices, 0), axis=seg_rows.ndim - 1)
    return indices - latest


def rope_tables(positions, head_dim):
    halves = head_dim // 2
    frequency = base_theta ** (-2.0 * jnp.arange(halves, dtype=jnp.float32) / head_dim)
    angles = positions.astype(jnp.float32)[:, None] * frequency[None, :]
    angles = jnp.concatenate([angles, angles], axis=1)
    return (jnp.cos(angles)[:, None, :], jnp.sin(angles)[:, None, :])


def rotate(values, cos_table, sin_table):
    halves = values.shape[-1] // 2
    turned = jnp.concatenate([-values[..., halves:], values[..., :halves]], axis=-1)
    return values * cos_table + turned * sin_table


def rotate_back(grads, cos_table, sin_table):
    halves = grads.shape[-1] // 2
    scaled = grads * sin_table
    return grads * cos_table + jnp.concatenate(
        [scaled[..., halves:], -scaled[..., :halves]], axis=-1
    )


def masked_scores(queries, key_rows, seg_rows):
    length, kv_heads, head_dim = key_rows.shape
    grouped = queries.reshape(length, kv_heads, -1, head_dim)
    raw_scores = jnp.einsum(
        "qhgd,khd->hgqk", grouped, key_rows, preferred_element_type=jnp.float32
    ) * head_dim ** (-0.5)
    indices = jnp.arange(length)
    allowed = (indices[:, None] >= indices[None, :]) & (seg_rows[:, None] == seg_rows[None, :])
    return (jnp.where(allowed, raw_scores, -1e30), grouped)


def attend_forward(seq_item):
    queries, key_rows, value_rows, seg_rows = seq_item
    scores, grouped = masked_scores(queries, key_rows, seg_rows)
    highest = jnp.max(scores, axis=-1, keepdims=True)
    weights = jnp.exp(scores - highest)
    totals = jnp.sum(weights, axis=-1, keepdims=True)
    shares = (weights / totals).astype(jnp.bfloat16)
    attended = jnp.einsum("hgqk,khd->qhgd", shares, value_rows, preferred_element_type=jnp.float32)
    return (attended.reshape(queries.shape[0], -1), highest + jnp.log(totals))


def attend_backward(seq_item):
    queries, key_rows, value_rows, seg_rows, log_total, head_grad = seq_item
    scores, grouped = masked_scores(queries, key_rows, seg_rows)
    factor = key_rows.shape[2] ** (-0.5)
    shares = jnp.exp(scores - log_total)
    grad_grouped = head_grad.reshape(grouped.shape)
    share_grad = jnp.einsum(
        "qhgd,khd->hgqk", grad_grouped, value_rows, preferred_element_type=jnp.float32
    )
    row_dot = jnp.sum(shares * share_grad, axis=-1, keepdims=True)
    score_grad = (shares * (share_grad - row_dot)).astype(jnp.bfloat16)
    query_grad = (
        jnp.einsum("hgqk,khd->qhgd", score_grad, key_rows, preferred_element_type=jnp.float32)
        * factor
    )
    key_grad = (
        jnp.einsum("hgqk,qhgd->khd", score_grad, grouped, preferred_element_type=jnp.float32)
        * factor
    )
    value_grad = jnp.einsum(
        "hgqk,qhgd->khd",
        shares.astype(jnp.bfloat16),
        grad_grouped,
        preferred_element_type=jnp.float32,
    )
    return (query_grad.reshape(queries.shape[0], -1), key_grad, value_grad)


def dense_gates(logits, routes, expert_ids):
    hits = jnp.any(routes[:, :, None] == expert_ids[None, None, :], axis=1)
    chosen = jnp.where(hits, logits, -jnp.inf)
    weights = jnp.exp(chosen - jnp.max(chosen, axis=1, keepdims=True))
    return weights / jnp.sum(weights, axis=1, keepdims=True)


def shards(
    tokens,
    gain_attn,
    w_query,
    w_key,
    w_value,
    w_out,
    gain_ffn,
    w_router,
    w_gate,
    w_up,
    w_down,
    segment_ids,
    routes,
    out_grad,
):
    tok_rows, width = tokens.shape
    group_rows = segment_ids.shape[0]
    seq_len = SEQ_LEN
    seq_count = group_rows // seq_len
    query_cols = w_query.shape[1]
    kv_cols = w_key.shape[1]
    head_dim = HEAD
    tp_index = lax.axis_index("tp")
    expert_count = w_router.shape[1]
    capacity = CAP
    top_count = routes.shape[1]
    local_experts = w_gate.shape[0]
    owner_count = lax.axis_size("exp")
    gate_full, up_full, down_full = (
        lax.all_gather(w_gate, "tp", axis=2, tiled=True),
        lax.all_gather(w_up, "tp", axis=2, tiled=True),
        lax.all_gather(w_down, "tp", axis=1, tiled=True),
    )
    exp_index = lax.axis_index("exp")
    routes_all = lax.all_gather(routes, "exp", axis=0, tiled=True)
    og_all = lax.all_gather(out_grad, "exp", axis=0, tiled=True)
    own_ids = exp_index * local_experts + jnp.arange(local_experts, dtype=jnp.int32)
    own_hits = jnp.any(
        routes_all.T.reshape(1, top_count, owner_count, tok_rows) == own_ids[:, None, None, None],
        axis=1,
    )
    tok_ids = jnp.arange(tok_rows, dtype=jnp.int32)
    earlier = (tok_ids[:, None] < tok_ids[None, :]).astype(jnp.bfloat16)
    ranks = jnp.einsum(
        "usr,rt->ust", own_hits.astype(jnp.bfloat16), earlier, preferred_element_type=jnp.float32
    ).astype(jnp.int32)
    ranks = jnp.where(own_hits, ranks, -1)
    dispatch = (
        ranks[:, :, None, :] == jnp.arange(capacity, dtype=jnp.int32)[None, None, :, None]
    ).astype(jnp.bfloat16)
    og_packed = (
        jnp.einsum(
            "usct,std->uscd",
            dispatch,
            og_all.reshape(owner_count, tok_rows, width),
            preferred_element_type=jnp.float32,
        )
        .astype(jnp.bfloat16)
        .reshape(local_experts, -1, width)
    )
    source = tokens.astype(jnp.float32)
    scale_one = lax.rsqrt(jnp.mean(source * source, axis=1, keepdims=True) + epsilon)
    unit_one = source * scale_one
    normed = (unit_one * gain_attn).astype(jnp.bfloat16)
    gathered = lax.all_gather(normed, "tp", axis=0, tiled=True)
    w_proj = jnp.concatenate([w_query, w_key, w_value], axis=1)
    projected = jnp.dot(gathered, w_proj, preferred_element_type=jnp.float32)
    seq_rows = segment_ids.reshape(seq_count, seq_len)
    cos_table, sin_table = rope_tables(doc_positions(seq_rows).reshape(-1), head_dim)
    queries = rotate(
        projected[:, :query_cols].reshape(group_rows, -1, head_dim), cos_table, sin_table
    ).astype(jnp.bfloat16)
    key_rows = rotate(
        projected[:, query_cols : query_cols + kv_cols].reshape(group_rows, -1, head_dim),
        cos_table,
        sin_table,
    ).astype(jnp.bfloat16)
    value_rows = (
        projected[:, query_cols + kv_cols :].astype(jnp.bfloat16).reshape(group_rows, -1, head_dim)
    )
    query_seqs = queries.reshape(seq_count, seq_len, -1, head_dim)
    key_seqs = key_rows.reshape(seq_count, seq_len, -1, head_dim)
    value_seqs = value_rows.reshape(seq_count, seq_len, -1, head_dim)
    attended, log_total = lax.map(attend_forward, (query_seqs, key_seqs, value_seqs, seq_rows))
    head_rows = attended.reshape(group_rows, query_cols).astype(jnp.bfloat16)
    out_local = lax.dynamic_slice_in_dim(w_out, tp_index * query_cols, query_cols, 0)
    part_rows = head_rows
    branch = lax.psum_scatter(
        jnp.dot(part_rows, out_local, preferred_element_type=jnp.float32),
        "tp",
        scatter_dimension=0,
        tiled=True,
    )
    hidden = source + branch
    scale_two = lax.rsqrt(jnp.mean(hidden * hidden, axis=1, keepdims=True) + epsilon)
    unit_two = hidden * scale_two
    normed_ffn = (unit_two * gain_ffn).astype(jnp.bfloat16)
    logits = jnp.dot(normed_ffn, w_router, preferred_element_type=jnp.float32)
    expert_ids = jnp.arange(expert_count, dtype=jnp.int32)
    gates = dense_gates(logits, routes, expert_ids)
    x_all = lax.all_gather(normed_ffn, "exp", axis=0, tiled=True).reshape(
        owner_count, tok_rows, width
    )
    logits_all = jnp.einsum("std,de->ste", x_all, w_router, preferred_element_type=jnp.float32)
    gates_all = dense_gates(logits_all.reshape(-1, expert_count), routes_all, expert_ids).reshape(
        owner_count, tok_rows, owner_count, local_experts
    )
    own_gates = lax.dynamic_index_in_dim(gates_all, exp_index, 2, keepdims=False)
    slot_gates = jnp.einsum(
        "usct,stu->usc",
        dispatch,
        own_gates,
        precision=lax.Precision.HIGHEST,
        preferred_element_type=jnp.float32,
    )
    received = (
        jnp.einsum("usct,std->uscd", dispatch, x_all, preferred_element_type=jnp.float32)
        .astype(jnp.bfloat16)
        .reshape(local_experts, -1, width)
    )
    slot_gates = slot_gates.reshape(local_experts, -1)
    gate_pre = jnp.einsum("umd,udf->umf", received, gate_full, preferred_element_type=jnp.float32)
    up_pre = jnp.einsum("umd,udf->umf", received, up_full, preferred_element_type=jnp.float32)
    sigmoid_gate = jax.nn.sigmoid(gate_pre)
    inner_act = (gate_pre * sigmoid_gate * up_pre).astype(jnp.bfloat16)
    result = (
        jnp.einsum("umf,ufd->umd", inner_act, down_full, preferred_element_type=jnp.float32)
        .astype(jnp.bfloat16)
        .astype(jnp.float32)
    )
    weighted = (slot_gates[..., None] * result).astype(jnp.bfloat16)
    mixture_part = jnp.einsum(
        "usct,uscd->std",
        dispatch,
        weighted.reshape(local_experts, owner_count, capacity, width),
        preferred_element_type=jnp.float32,
    ).astype(jnp.bfloat16)
    mixture = lax.psum_scatter(
        mixture_part.reshape(-1, width), "exp", scatter_dimension=0, tiled=True
    ).astype(jnp.float32)
    output = (hidden + mixture).astype(jnp.bfloat16)
    share_slots = jnp.sum(result * og_packed.astype(jnp.float32), axis=2)
    share_back = jnp.einsum(
        "usct,usc->sut",
        dispatch,
        share_slots.reshape(local_experts, owner_count, capacity),
        precision=lax.Precision.HIGHEST,
        preferred_element_type=jnp.float32,
    )
    share_grad = (
        lax.all_to_all(share_back, "exp", split_axis=0, concat_axis=0, tiled=True)
        .reshape(expert_count, tok_rows)
        .T
    )
    arrived = (slot_gates[..., None] * og_packed.astype(jnp.float32)).astype(jnp.bfloat16)
    inner_grad = jnp.einsum("umd,ufd->umf", arrived, down_full, preferred_element_type=jnp.float32)
    gate_grad = (
        inner_grad * up_pre * sigmoid_gate * (1.0 + gate_pre * (1.0 - sigmoid_gate))
    ).astype(jnp.bfloat16)
    up_grad = (inner_grad * gate_pre * sigmoid_gate).astype(jnp.bfloat16)
    back_rows = (
        jnp.einsum("umf,udf->umd", gate_grad, gate_full, preferred_element_type=jnp.float32)
        + jnp.einsum("umf,udf->umd", up_grad, up_full, preferred_element_type=jnp.float32)
    ).astype(jnp.bfloat16)
    grad_part = jnp.einsum(
        "usct,uscd->std",
        dispatch,
        back_rows.reshape(local_experts, owner_count, capacity, width),
        preferred_element_type=jnp.float32,
    ).astype(jnp.bfloat16)
    ffn_grad = lax.psum_scatter(
        grad_part.reshape(-1, width), "exp", scatter_dimension=0, tiled=True
    ).astype(jnp.float32)
    down_part = jnp.einsum("umf,umd->ufd", inner_act, arrived, preferred_element_type=jnp.float32)
    gate_part = jnp.einsum("umd,umf->udf", received, gate_grad, preferred_element_type=jnp.float32)
    up_part = jnp.einsum("umd,umf->udf", received, up_grad, preferred_element_type=jnp.float32)
    logit_grad = (gates * (share_grad - jnp.sum(gates * share_grad, axis=1, keepdims=True))).astype(
        jnp.bfloat16
    )
    router_part = contract(normed_ffn, logit_grad, 0, 0)
    ffn_grad = ffn_grad + contract(logit_grad, w_router, 1, 1)
    ffn_part = jnp.sum(ffn_grad * unit_two, axis=0)
    unit_grad_two = ffn_grad * gain_ffn
    hidden_grad = out_grad.astype(jnp.float32) + scale_two * (
        unit_grad_two - unit_two * jnp.mean(unit_grad_two * unit_two, axis=1, keepdims=True)
    )
    branch_low = hidden_grad.astype(jnp.bfloat16)
    part_rows = lax.all_gather(branch_low, "tp", axis=0, tiled=True)
    update = contract(part_rows, out_local, 1, 1)
    grads_heads = update
    grads_heads, out_rows = (grads_heads, contract(head_rows, part_rows, 0, 0))
    head_grad = grads_heads.astype(jnp.bfloat16)
    out_weight_grad = lax.all_gather(
        lax.psum(out_rows.astype(jnp.bfloat16), "exp"), "tp", axis=0, tiled=True
    ).astype(jnp.float32)
    query_grad, key_grad, value_grad = lax.map(
        attend_backward,
        (
            query_seqs,
            key_seqs,
            value_seqs,
            seq_rows,
            log_total,
            head_grad.reshape(seq_count, seq_len, query_cols),
        ),
    )
    query_grad = rotate_back(query_grad.reshape(group_rows, -1, head_dim), cos_table, sin_table)
    key_grad = rotate_back(key_grad.reshape(group_rows, -1, head_dim), cos_table, sin_table)
    proj_grad = jnp.concatenate(
        [
            query_grad.reshape(group_rows, -1),
            key_grad.reshape(group_rows, -1),
            value_grad.reshape(group_rows, -1),
        ],
        axis=1,
    ).astype(jnp.bfloat16)
    proj_part = contract(gathered, proj_grad, 0, 0)
    part_rows = proj_grad
    normed_grad = lax.psum_scatter(
        contract(part_rows, w_proj, 1, 1).astype(jnp.bfloat16),
        "tp",
        scatter_dimension=0,
        tiled=True,
    ).astype(jnp.float32)
    attn_part = jnp.sum(normed_grad * unit_one, axis=0)
    unit_grad_one = normed_grad * gain_attn
    input_grad = hidden_grad + scale_one * (
        unit_grad_one - unit_one * jnp.mean(unit_grad_one * unit_one, axis=1, keepdims=True)
    )
    gate_weight_grad, up_weight_grad, down_weight_grad = (
        lax.psum_scatter(
            gate_part.astype(jnp.bfloat16), "tp", scatter_dimension=2, tiled=True
        ).astype(jnp.float32),
        lax.psum_scatter(
            up_part.astype(jnp.bfloat16), "tp", scatter_dimension=2, tiled=True
        ).astype(jnp.float32),
        lax.psum_scatter(
            down_part.astype(jnp.bfloat16), "tp", scatter_dimension=1, tiled=True
        ).astype(jnp.float32),
    )
    query_weight_grad, key_weight_grad, value_weight_grad = (
        lax.psum(proj_part[:, :query_cols].astype(jnp.bfloat16), "exp").astype(jnp.float32),
        lax.psum(
            proj_part[:, query_cols : query_cols + kv_cols].astype(jnp.bfloat16), "exp"
        ).astype(jnp.float32),
        lax.psum(proj_part[:, query_cols + kv_cols :].astype(jnp.bfloat16), "exp").astype(
            jnp.float32
        ),
    )
    attn_gain_grad, ffn_gain_grad, router_grad = lax.psum(
        (attn_part, ffn_part, router_part), ("exp", "tp")
    )
    return (
        output,
        input_grad,
        attn_gain_grad,
        query_weight_grad,
        key_weight_grad,
        value_weight_grad,
        out_weight_grad,
        ffn_gain_grad,
        router_grad,
        gate_weight_grad,
        up_weight_grad,
        down_weight_grad,
    )


def solution(mesh):
    in_specs = (
        P(("exp", "tp"), None),
        P(),
        P(None, "tp"),
        P(None, "tp"),
        P(None, "tp"),
        P(),
        P(),
        P(),
        P("exp", None, "tp"),
        P("exp", None, "tp"),
        P("exp", "tp", None),
        P("exp"),
        P(("exp", "tp"), None),
        P(("exp", "tp"), None),
    )
    out_specs = (
        P(("exp", "tp"), None),
        P(("exp", "tp"), None),
        P(),
        P(None, "tp"),
        P(None, "tp"),
        P(None, "tp"),
        P(),
        P(),
        P(),
        P("exp", None, "tp"),
        P("exp", None, "tp"),
        P("exp", "tp", None),
    )
    return jax.shard_map(shards, mesh=mesh, in_specs=in_specs, out_specs=out_specs, check_vma=False)
```

profile of v0, /device:TPU:0, one launch (start us, length us, event | category | flops | bytes accessed | tf_op | source)
XLA Modules:
  0.0 934.5 jit_solution(1334416880597368355)
XLA Ops:
  24.3 11.9 %all-gather.9.cloned.1.call-done = bf16[512,1024]{1,0:T(8,128)(2,1)} async-done(((bf16[256,1024]{1,0:T(8,128)(2,1)}), bf16[512,1024]{1,0:T(8,128)(2,1)}) %all-gather.9.cloned.1.call-update) | async-done | bytes 1048592 | tf_op jit(solution)/shard_map/all_gather | solution.py:171
  61.8 31.3 %reduce-scatter.8.cloned.1.call-done = f32[256,1024]{1,0:T(8,128)} async-done(((f32[512,1024]{1,0:T(8,128)}), f32[256,1024]{1,0:T(8,128)}) %reduce-scatter.8.cloned.1.call-update) | async-done | bytes 1048592 | tf_op jit(solution)/shard_map/reduce_scatter | solution.py:194
  97.9 22.7 %all_gather.28 = s32[4096,8]{0,1:T(8,128)S(1)} all-gather(s32[256,8]{0,1:T(8,128)S(1)} %copy-done.24), channel_id=1, replica_groups=mesh['exp'=16,'tp'=2] {'exp'}, dimensions={0}, use_global_device_ids=true | all-gather | bytes 139264 | tf_op jit(solution)/shard_map/all_gather | solution.py:141
  122.2 17.5 %all-gather.19.cloned.1.call-done = bf16[4096,1024]{1,0:T(8,128)(2,1)} async-done(((bf16[256,1024]{1,0:T(8,128)(2,1)}), bf16[4096,1024]{1,0:T(8,128)(2,1)}) %all-gather.19.cloned.1.call-update) | async-done | bytes 8388624 | tf_op jit(solution)/shard_map/all_gather | solution.py:142
  152.8 62.6 %all-gather.11.cloned.1.call-done = bf16[4096,1024]{1,0:T(8,128)(2,1)} async-done(((bf16[256,1024]{1,0:T(8,128)(2,1)}), bf16[4096,1024]{1,0:T(8,128)(2,1)}) %all-gather.11.cloned.1.call-update) | async-done | bytes 8388624 | tf_op jit(solution)/shard_map/all_gather | solution.py:207
  248.3 11.7 %fusion.82 = f32[2,2048,512]{2,1,0:T(8,128)} fusion(bf16[2,2048,1024]{2,1,0:T(8,128)(2,1)} %bitcast.198, bf16[2,1024,512]{2,1,0:T(8,128)(2,1)} %all-gather.13.cloned.1.call-done), kind=kOutput, calls=%fused_computation.164 | convolution fusion | flops 4294967296 | bytes 18874368 | tf_op jit(solution)/shard_map/umd,udf->umf/dot_general | solution.py:228
  260.0 22.8 %all-gather.15.cloned.1.call-done = bf16[2,1024,512]{2,1,0:T(8,128)(2,1)} async-done(((bf16[2,1024,256]{2,1,0:T(8,128)(2,1)}), bf16[2,1024,512]{2,1,0:T(8,128)(2,1)}) %all-gather.15.cloned.1.call-update) | async-done | bytes 2097168 | tf_op jit(solution)/shard_map/all_gather | solution.py:137
  282.9 11.8 %fusion.83 = f32[2,2048,512]{2,1,0:T(8,128)} fusion(bf16[2,2048,1024]{2,1,0:T(8,128)(2,1)} %bitcast.199, bf16[2,1024,512]{2,1,0:T(8,128)(2,1)} %all-gather.15.cloned.1.call-done), kind=kOutput, calls=%fused_computation.165 | convolution fusion | flops 4294967296 | bytes 18874368 | tf_op jit(solution)/shard_map/umd,udf->umf/dot_general | solution.py:229
  294.7 9.1 fusion.2
  303.8 13.7 %all-gather.17.cloned.1.call-done = bf16[2,512,1024]{2,1,0:T(8,128)(2,1)} async-done(((bf16[2,256,1024]{2,1,0:T(8,128)(2,1)}), bf16[2,512,1024]{2,1,0:T(8,128)(2,1)}) %all-gather.17.cloned.1.call-update) | async-done | bytes 2097168 | tf_op jit(solution)/shard_map/all_gather | solution.py:138
  317.5 16.8 %multiply_convert_fusion = (bf16[2,2048,512]{2,1,0:T(8,128)(2,1)}, bf16[2,2048,512]{2,1,0:T(8,128)(2,1)}, bf16[2,2048,512]{2,1,0:T(8,128)(2,1)}) fusion(f32[2,2048,512]{2,1,0:T(8,128)} %fusion.82, f32[2,2048,512]{2,1,0:T(8,128)} %fusion.83, bf16[2,2048,1024]{2,1,0:T(8,128)(2,1)} %fusion.2, bf16[2,512,1024]{2,1,0:T(8,128)(2,1)} %all-gather.17.cloned.1.call-done), kind=kOutput, calls=%fused_computation.19 | convolution fusion | flops 4328521728 | bytes 39845888 | tf_op jit(solution)/shard_map/umd,ufd->umf/dot_general | solution.py:262
  334.3 10.4 %fusion.84 = f32[2,2048,1024]{2,1,0:T(8,128)} fusion(bf16[2,2048,512]{2,1,0:T(8,128)(2,1)} %get-tuple-element.76, bf16[2,1024,512]{2,1,0:T(8,128)(2,1)S(1)} %copy-done.31), kind=kOutput, calls=%fused_computation.166 | convolution fusion | flops 4294967296 | bytes 23068672 | tf_op jit(solution)/shard_map/umf,udf->umd/dot_general | solution.py:268
  344.7 15.4 %add_convert_fusion = bf16[2,2048,1024]{2,1,0:T(8,128)(2,1)} fusion(f32[2,2048,1024]{2,1,0:T(8,128)} %fusion.84, bf16[2,2048,512]{2,1,0:T(8,128)(2,1)} %get-tuple-element.75, bf16[2,1024,512]{2,1,0:T(8,128)(2,1)} %all-gather.15.cloned.1.call-done), kind=kOutput, calls=%fused_computation.9 | convolution fusion | flops 4303355904 | bytes 31457280 | tf_op jit(solution)/shard_map/umf,udf->umd/dot_general | solution.py:269
  369.5 14.9 %fusion.1 = (f32[2,2048]{1,0:T(2,128)S(1)}, bf16[2,2048,1024]{2,1,0:T(8,128)(2,1)}) fusion(f32[2,16,128,1024]{3,2,1,0:T(8,128)} %copy.82, f32[2,2048]{1,0:T(2,128)S(1)} %bitcast.223, bf16[2,2048,512]{2,1,0:T(8,128)(2,1)} %get-tuple-element.77, bf16[2,512,1024]{2,1,0:T(8,128)(2,1)} %all-gather.17.cloned.1.call-done), kind=kOutput, calls=%fused_computation.3 | convolution fusion | flops 4320129024 | bytes 31490048 | tf_op jit(solution)/shard_map/umf,ufd->umd/dot_general | solution.py:233
  403.2 67.0 %reduce-scatter.12.cloned.1.call-done = bf16[256,1024]{1,0:T(8,128)(2,1)} async-done(((bf16[4096,1024]{1,0:T(8,128)(2,1)}), bf16[256,1024]{1,0:T(8,128)(2,1)}) %reduce-scatter.12.cloned.1.call-update) | async-done | bytes 524304 | tf_op jit(solution)/shard_map/reduce_scatter | solution.py:277
  475.9 20.3 %all-gather.21.cloned.1.call-done = bf16[512,1024]{1,0:T(8,128)(2,1)} async-done(((bf16[256,1024]{1,0:T(8,128)(2,1)}), bf16[512,1024]{1,0:T(8,128)(2,1)}) %all-gather.21.cloned.1.call-update) | async-done | bytes 1048592 | tf_op jit(solution)/shard_map/all_gather | solution.py:294
  516.4 10.5 %convolution_convert_fusion.1 = bf16[2,512,1024]{2,1,0:T(8,128)(2,1)} fusion(bf16[2,2048,512]{2,1,0:T(8,128)(2,1)} %get-tuple-element.77, bf16[2,2048,1024]{2,1,0:T(8,128)(2,1)} %fusion.2), kind=kOutput, calls=%fused_computation.44 | convolution fusion | flops 4296015872 | bytes 14680064 | tf_op jit(solution)/shard_map/umf,umd->ufd/dot_general | solution.py:280
  527.2 10.5 %convolution_convert_fusion.3 = bf16[2,1024,512]{2,1,0:T(8,128)(2,1)} fusion(bf16[2,2048,1024]{2,1,0:T(8,128)(2,1)} %bitcast.200, bf16[2,2048,512]{2,1,0:T(8,128)(2,1)} %get-tuple-element.76), kind=kOutput, calls=%fused_computation.46 | convolution fusion | flops 4296015872 | bytes 14680064 | tf_op jit(solution)/shard_map/umd,umf->udf/dot_general | solution.py:281
  537.9 10.6 %convolution_convert_fusion.2 = bf16[2,1024,512]{2,1,0:T(8,128)(2,1)} fusion(bf16[2,2048,1024]{2,1,0:T(8,128)(2,1)} %bitcast.201, bf16[2,2048,512]{2,1,0:T(8,128)(2,1)} %get-tuple-element.75), kind=kOutput, calls=%fused_computation.45 | convolution fusion | flops 4296015872 | bytes 14680064 | tf_op jit(solution)/shard_map/umd,umf->udf/dot_general | solution.py:282
  559.9 60.4 %all-reduce.7.cloned.1.call-done = (bf16[1024,512]{1,0:T(8,128)(2,1)}, bf16[1024,256]{1,0:T(8,128)(2,1)}, bf16[1024,256]{1,0:T(8,128)(2,1)}, bf16[512,1024]{1,0:T(8,128)(2,1)}) async-done(((bf16[1024,512]{1,0:T(8,128)(2,1)}, bf16[1024,256]{1,0:T(8,128)(2,1)}, bf16[1024,256]{1,0:T(8,128)(2,1)}, bf16[512,1024]{1,0:T(8,128)(2,1)}), (bf16[1024,512]{1,0:T(8,128)(2,1)}, bf16[1024,256]{1,0:T(8,128)(2,1)}, ...) | async-done | bytes 3145744 | tf_op jit(solution)/shard_map/psum | solution.py:348
  637.9 13.4 %reduce-scatter.14.cloned.1.call-done = bf16[256,1024]{1,0:T(8,128)(2,1)} async-done(((bf16[512,1024]{1,0:T(8,128)(2,1)}), bf16[256,1024]{1,0:T(8,128)(2,1)}) %reduce-scatter.14.cloned.1.call-update) | async-done | bytes 524304 | tf_op jit(solution)/shard_map/reduce_scatter | solution.py:325
  653.0 107.7 %reduce-scatter.10.cloned.1.call-done = bf16[256,1024]{1,0:T(8,128)(2,1)} async-done(((bf16[4096,1024]{1,0:T(8,128)(2,1)}), bf16[256,1024]{1,0:T(8,128)(2,1)}) %reduce-scatter.10.cloned.1.call-update) | async-done | bytes 524304 | tf_op jit(solution)/shard_map/reduce_scatter | solution.py:244
  764.2 40.5 %all-reduce = (f32[1024]{0:T(1024)}, f32[1024]{0:T(1024)}) all-reduce(f32[1024]{0:T(1024)S(1)} %get-tuple-element.55, f32[1024]{0:T(1024)S(1)} %get-tuple-element.53), channel_id=1, replica_groups=mesh['exp'=16,'tp'=2] {'exp','tp'}, use_global_device_ids=true, to_apply=%region_23.24 | all-reduce | flops 2048 | bytes 16384 | tf_op jit(solution)/shard_map/psum | solution.py:356
  808.8 116.2 %all-reduce.5.cloned.1.call-done = f32[1024,32]{0,1:T(8,128)} async-done(((f32[1024,32]{0,1:T(8,128)}), f32[1024,32]{0,1:T(8,128)}) %all-reduce.5.cloned.1.call-update) | async-done | bytes 131088 | tf_op jit(solution)/shard_map/psum | solution.py:356
  (210 shorter events, 187.7 us)
Async XLA Ops:
  8.0 51.1 %copy-start = (bf16[1024,1024]{1,0:T(8,128)(2,1)S(1)}, bf16[1024,1024]{1,0:T(8,128)(2,1)}, u32[]{:S(2)}) copy-start(bf16[1024,1024]{1,0:T(8,128)(2,1)} %param.19) | copy-start | bytes 6291460
  8.0 28.2 %all-gather.9.cloned.1.call-start = ((), (), s32[]{:S(2)}) async-start(), calls=%async_computation.8 | async-start | bytes 1572864 | tf_op jit(solution)/shard_map/all_gather | solution.py:171
  12.0 81.1 %reduce-scatter.8.cloned.1.call-start = ((), (), s32[]{:S(2)}) async-start(), calls=%async_computation.9 | async-start | bytes 3145728 | tf_op jit(solution)/shard_map/reduce_scatter | solution.py:194
  58.3 36.5 %copy-start.20 = (f32[1024]{0:T(1024)S(1)}, f32[1024]{0:T(1024)}, u32[]{:S(2)}) copy-start(f32[1024]{0:T(1024)} %param.20) | copy-start | bytes 12292
  58.3 39.6 %copy-start.24 = (s32[256,8]{0,1:T(8,128)S(1)}, s32[256,8]{0,1:T(8,128)}, u32[]{:S(2)}) copy-start(s32[256,8]{0,1:T(8,128)} %param.26) | copy-start | bytes 24580
  61.2 78.6 %all-gather.19.cloned.1.call-start = ((), (), s32[]{:S(2)}) async-start(), calls=%async_computation.15 | async-start | bytes 8912896 | tf_op jit(solution)/shard_map/all_gather | solution.py:142
  61.7 153.7 %all-gather.11.cloned.1.call-start = ((), (), s32[]{:S(2)}) async-start(), calls=%async_computation.10 | async-start | bytes 8912896 | tf_op jit(solution)/shard_map/all_gather | solution.py:207
  95.7 152.6 %all-gather.13.cloned.1.call-start = ((), (), s32[]{:S(2)}) async-start(), calls=%async_computation.11 | async-start | bytes 3145728 | tf_op jit(solution)/shard_map/all_gather | solution.py:136
  96.3 186.6 %all-gather.15.cloned.1.call-start = ((), (), s32[]{:S(2)}) async-start(), calls=%async_computation.12 | async-start | bytes 3145728 | tf_op jit(solution)/shard_map/all_gather | solution.py:137
  97.0 220.5 %all-gather.17.cloned.1.call-start = ((), (), s32[]{:S(2)}) async-start(), calls=%async_computation.13 | async-start | bytes 3145728 | tf_op jit(solution)/shard_map/all_gather | solution.py:138
  97.8 372.4 %reduce-scatter.12.cloned.1.call-start = ((), (), s32[]{:S(2)}) async-start(), calls=%async_computation.16 | async-start | bytes 8912896 | tf_op jit(solution)/shard_map/reduce_scatter | solution.py:277
  146.7 68.7 %copy-start.13 = (bf16[1024,32]{0,1:T(8,128)(2,1)S(1)}, bf16[1024,32]{0,1:T(8,128)(2,1)}, u32[]{:S(2)}) copy-start(bf16[1024,32]{0,1:T(8,128)(2,1)} %param.21) | copy-start | bytes 196612
  387.9 12.2 %all-to-all-start = ((f32[16,2,256]{2,1,0:T(2,128)}), f32[16,2,256]{2,1,0:T(2,128)}, u32[]{:S(2)}, u32[]{:S(2)}) async-start(f32[16,2,256]{2,1,0:T(2,128)} %bitcast.225), calls=%async_computation.3 | async-start | bytes 65536 | tf_op jit(solution)/shard_map/all_to_all | solution.py:257
  393.5 102.7 %all-gather.21.cloned.1.call-start = ((), (), s32[]{:S(2)}) async-start(), calls=%async_computation.17 | async-start | bytes 1572864 | tf_op jit(solution)/shard_map/all_gather | solution.py:294
  475.1 145.2 %all-reduce.7.cloned.1.call-start = ((), (), s32[]{:S(2)}) async-start(), calls=%async_computation.24 | async-start | bytes 6291456 | tf_op jit(solution)/shard_map/psum | solution.py:348
  516.4 106.3 %reduce-scatter.20.cloned.1.call-start = ((), (), s32[]{:S(2)}) async-start(), calls=%async_computation.23 | async-start | bytes 3145728 | tf_op jit(solution)/shard_map/reduce_scatter | solution.py:343
  526.9 98.5 %reduce-scatter.16.cloned.1.call-start = ((), (), s32[]{:S(2)}) async-start(), calls=%async_computation.21 | async-start | bytes 3145728 | tf_op jit(solution)/shard_map/reduce_scatter | solution.py:337
  537.8 90.4 %reduce-scatter.18.cloned.1.call-start = ((), (), s32[]{:S(2)}) async-start(), calls=%async_computation.22 | async-start | bytes 3145728 | tf_op jit(solution)/shard_map/reduce_scatter | solution.py:340
  548.5 102.8 %reduce-scatter.14.cloned.1.call-start = ((), (), s32[]{:S(2)}) async-start(), calls=%async_computation.18 | async-start | bytes 1572864 | tf_op jit(solution)/shard_map/reduce_scatter | solution.py:325
  552.7 208.0 %reduce-scatter.10.cloned.1.call-start = ((), (), s32[]{:S(2)}) async-start(), calls=%async_computation.14 | async-start | bytes 8912896 | tf_op jit(solution)/shard_map/reduce_scatter | solution.py:244
  559.9 244.9 %all-gather.23.cloned.1.call-start = ((), (), s32[]{:S(2)}) async-start(), calls=%async_computation.19 | async-start | bytes 3145728 | tf_op jit(solution)/shard_map/all_gather | solution.py:299
  620.4 304.6 %all-reduce.5.cloned.1.call-start = ((), (), s32[]{:S(2)}) async-start(), calls=%async_computation.20 | async-start | bytes 262144 | tf_op jit(solution)/shard_map/psum | solution.py:356
  622.6 138.1 %copy-start.21 = (f32[1024]{0:T(1024)S(1)}, f32[1024]{0:T(1024)}, u32[]{:S(2)}) copy-start(f32[1024]{0:T(1024)} %param.20) | copy-start | bytes 12292
  622.6 138.1 %copy-start.27 = (f32[256]{0:T(256)S(1)}, f32[256]{0:T(256)}, u32[]{:S(2)}) copy-start(f32[256]{0:T(256)} %copy-done.26) | copy-start | bytes 3076
  (30 other events, 205.2 us)
Sparse Core Ops, SparseCore 0:
  12.2 23.9 all-gather.8
  61.3 31.8 reduce-scatter.7
  475.2 20.9 all-gather.20
  527.1 31.8 reduce-scatter.19
  561.6 31.8 reduce-scatter.15
  596.2 31.8 reduce-scatter.17
  631.0 20.3 reduce-scatter.13
  655.9 104.7 reduce-scatter.9
  762.3 33.3 all-gather.22
  802.5 122.3 all-reduce.4
Sparse Core Ops, SparseCore 1:
  64.0 75.6 all-gather.18
  142.6 72.8 all-gather.10
  216.9 31.3 all-gather.12
  249.9 32.9 all-gather.14
  284.5 32.9 all-gather.16
  366.9 103.2 reduce-scatter.11
  516.4 103.8 all-reduce.6
where the time goes:
time: 943 us; the launch traced here: 934 us
  waiting for transfers between devices  563 us (60%)
  matrix products  185 us (20%)
  blocking collectives  63.2 us (7%)
  other arithmetic  61.6 us (7%)
  local copies, waits for them, and re-layouts  38.7 us (4%)
  between operations  16.9 us (2%)
    psum x1, waiting for transfers between devices, shards(): lax.psum((attn_part, ffn_part, router_part), ('exp', 'tp'))  116 us
    reduce_scatter x1, waiting for transfers between devices, shards(): lax.psum_scatter(mixture_part.reshape(-1, width), 'exp', scatter_dimensio...  108 us
    reduce_scatter x1, waiting for transfers between devices, shards(): lax.psum_scatter(grad_part.reshape(-1, width), 'exp', scatter_dimension=0...  67 us
    all_gather x1, waiting for transfers between devices, shards(): lax.all_gather(normed_ffn, 'exp', axis=0, tiled=True)  62.6 us
    psum x1, waiting for transfers between devices, shards(): lax.psum(proj_part[:, :query_cols].astype(jnp.bfloat16), 'exp')  60.4 us
    psum x1, blocking collectives, shards(): lax.psum((attn_part, ffn_part, router_part), ('exp', 'tp'))  40.5 us
    reduce_scatter x1, waiting for transfers between devices, shards(): lax.psum_scatter(jnp.dot(part_rows, out_local, preferred_element_type=jnp...  31.3 us
    all_gather x1, waiting for transfers between devices, shards(): lax.all_gather(w_up, 'tp', axis=2, tiled=True)  22.8 us
  transfers between devices with their start and end apart: 18, of which 14 were waited for; matrix products, arithmetic and copies ran while one was open for 19% of the time, Pallas kernels for 0%

commit v1 on v0

--- a/solution.py
+++ b/solution.py
@@ -354,7 +354,7 @@
         ),
     )
     attn_gain_grad, ffn_gain_grad, router_grad = lax.psum(
-        (attn_part, ffn_part, router_part), ("exp", "tp")
+        lax.psum((attn_part, ffn_part, router_part), "tp"), "exp"
     )
     return (
         output,

time: 943 us -> 908 us (0.963)
  waiting for transfers between devices: 563 us -> 529 us
    reduce_scatter x1, waiting for transfers between devices: 108 us -> 92.7 us  [shards(): lax.psum_scatter(mixture_part.reshape(-1, width), 'exp', scatter_dimensio...]
    reduce_scatter x1, waiting for transfers between devices: 13.4 us -> 0.01 us  [shards(): lax.psum_scatter(contract(part_rows, w_proj, 1, 1).astype(jnp.bfloat16),...]
    psum x1 -> x2, blocking collectives: 40.5 us -> 37.1 us  [the longest x1 32.1 us: shards(): lax.psum(lax.psum((attn_part, ffn_part, router_part), 'tp'), 'exp')]
    psum x1 -> x2, waiting for transfers between devices: 116 us -> 113 us  [the longest x1 80.5 us: shards(): lax.psum(lax.psum((attn_part, ffn_part, router_part), 'tp'), 'exp')]
  transfers between devices with their start and end apart: 18 -> 19, of which waited for: 14 -> 14; matrix products, arithmetic and copies ran while one was open for 19% -> 20% of each run, Pallas kernels for 0% -> 0%
where the time goes in v1:
time: 908 us; the launch traced here: 898 us
  waiting for transfers between devices  529 us (58%)
  matrix products  185 us (20%)
  other arithmetic  61.7 us (7%)
  blocking collectives  59.8 us (7%)
  local copies, waits for them, and re-layouts  38.8 us (4%)
  between operations  16.9 us (2%)
    reduce_scatter x1, waiting for transfers between devices, shards(): lax.psum_scatter(mixture_part.reshape(-1, width), 'exp', scatter_dimensio...  92.7 us
    psum x1, waiting for transfers between devices, shards(): lax.psum(lax.psum((attn_part, ffn_part, router_part), 'tp'), 'exp')  80.5 us
    reduce_scatter x1, waiting for transfers between devices, shards(): lax.psum_scatter(grad_part.reshape(-1, width), 'exp', scatter_dimension=0...  67.2 us
    all_gather x1, waiting for transfers between devices, shards(): lax.all_gather(normed_ffn, 'exp', axis=0, tiled=True)  62.6 us
    psum x1, waiting for transfers between devices, shards(): lax.psum(proj_part[:, :query_cols].astype(jnp.bfloat16), 'exp')  58.2 us
    psum x1, waiting for transfers between devices, shards(): lax.psum((attn_part, ffn_part, router_part), 'tp')  32.8 us
    psum x1, blocking collectives, shards(): lax.psum(lax.psum((attn_part, ffn_part, router_part), 'tp'), 'exp')  32.1 us
    reduce_scatter x1, waiting for transfers between devices, shards(): lax.psum_scatter(jnp.dot(part_rows, out_local, preferred_element_type=jnp...  31.3 us
  transfers between devices with their start and end apart: 19, of which 14 were waited for; matrix products, arithmetic and copies ran while one was open for 20% of the time, Pallas kernels for 0%

profile of v1, /device:TPU:0, one launch (start us, length us, event | category | flops | bytes accessed | tf_op | source)
XLA Modules:
  0.0 898.2 jit_solution(17429623348385578509)
XLA Ops:
  24.4 11.9 %all-gather.9.cloned.1.call-done = bf16[512,1024]{1,0:T(8,128)(2,1)} async-done(((bf16[256,1024]{1,0:T(8,128)(2,1)}), bf16[512,1024]{1,0:T(8,128)(2,1)}) %all-gather.9.cloned.1.call-update) | async-done | bytes 1048592 | tf_op jit(solution)/shard_map/all_gather | solution.py:171
  61.9 31.3 %reduce-scatter.8.cloned.1.call-done = f32[256,1024]{1,0:T(8,128)} async-done(((f32[512,1024]{1,0:T(8,128)}), f32[256,1024]{1,0:T(8,128)}) %reduce-scatter.8.cloned.1.call-update) | async-done | bytes 1048592 | tf_op jit(solution)/shard_map/reduce_scatter | solution.py:194
  97.9 22.7 %all_gather.28 = s32[4096,8]{0,1:T(8,128)S(1)} all-gather(s32[256,8]{0,1:T(8,128)S(1)} %copy-done.24), channel_id=1, replica_groups=mesh['exp'=16,'tp'=2] {'exp'}, dimensions={0}, use_global_device_ids=true | all-gather | bytes 139264 | tf_op jit(solution)/shard_map/all_gather | solution.py:141
  122.3 17.5 %all-gather.19.cloned.1.call-done = bf16[4096,1024]{1,0:T(8,128)(2,1)} async-done(((bf16[256,1024]{1,0:T(8,128)(2,1)}), bf16[4096,1024]{1,0:T(8,128)(2,1)}) %all-gather.19.cloned.1.call-update) | async-done | bytes 8388624 | tf_op jit(solution)/shard_map/all_gather | solution.py:142
  152.9 62.6 %all-gather.11.cloned.1.call-done = bf16[4096,1024]{1,0:T(8,128)(2,1)} async-done(((bf16[256,1024]{1,0:T(8,128)(2,1)}), bf16[4096,1024]{1,0:T(8,128)(2,1)}) %all-gather.11.cloned.1.call-update) | async-done | bytes 8388624 | tf_op jit(solution)/shard_map/all_gather | solution.py:207
  239.3 9.1 %all-gather.13.cloned.1.call-done = bf16[2,1024,512]{2,1,0:T(8,128)(2,1)} async-done(((bf16[2,1024,256]{2,1,0:T(8,128)(2,1)}), bf16[2,1024,512]{2,1,0:T(8,128)(2,1)}) %all-gather.13.cloned.1.call-update) | async-done | bytes 2097168 | tf_op jit(solution)/shard_map/all_gather | solution.py:136
  248.3 11.7 %fusion.82 = f32[2,2048,512]{2,1,0:T(8,128)} fusion(bf16[2,2048,1024]{2,1,0:T(8,128)(2,1)} %bitcast.198, bf16[2,1024,512]{2,1,0:T(8,128)(2,1)} %all-gather.13.cloned.1.call-done), kind=kOutput, calls=%fused_computation.164 | convolution fusion | flops 4294967296 | bytes 18874368 | tf_op jit(solution)/shard_map/umd,udf->umf/dot_general | solution.py:228
  260.1 22.9 %all-gather.15.cloned.1.call-done = bf16[2,1024,512]{2,1,0:T(8,128)(2,1)} async-done(((bf16[2,1024,256]{2,1,0:T(8,128)(2,1)}), bf16[2,1024,512]{2,1,0:T(8,128)(2,1)}) %all-gather.15.cloned.1.call-update) | async-done | bytes 2097168 | tf_op jit(solution)/shard_map/all_gather | solution.py:137
  282.9 11.8 %fusion.83 = f32[2,2048,512]{2,1,0:T(8,128)} fusion(bf16[2,2048,1024]{2,1,0:T(8,128)(2,1)} %bitcast.199, bf16[2,1024,512]{2,1,0:T(8,128)(2,1)} %all-gather.15.cloned.1.call-done), kind=kOutput, calls=%fused_computation.165 | convolution fusion | flops 4294967296 | bytes 18874368 | tf_op jit(solution)/shard_map/umd,udf->umf/dot_general | solution.py:229
  303.8 13.7 %all-gather.17.cloned.1.call-done = bf16[2,512,1024]{2,1,0:T(8,128)(2,1)} async-done(((bf16[2,256,1024]{2,1,0:T(8,128)(2,1)}), bf16[2,512,1024]{2,1,0:T(8,128)(2,1)}) %all-gather.17.cloned.1.call-update) | async-done | bytes 2097168 | tf_op jit(solution)/shard_map/all_gather | solution.py:138
  317.5 16.8 %multiply_convert_fusion = (bf16[2,2048,512]{2,1,0:T(8,128)(2,1)}, bf16[2,2048,512]{2,1,0:T(8,128)(2,1)}, bf16[2,2048,512]{2,1,0:T(8,128)(2,1)}) fusion(f32[2,2048,512]{2,1,0:T(8,128)} %fusion.82, f32[2,2048,512]{2,1,0:T(8,128)} %fusion.83, bf16[2,2048,1024]{2,1,0:T(8,128)(2,1)} %fusion.2, bf16[2,512,1024]{2,1,0:T(8,128)(2,1)} %all-gather.17.cloned.1.call-done), kind=kOutput, calls=%fused_computation.19 | convolution fusion | flops 4328521728 | bytes 39845888 | tf_op jit(solution)/shard_map/umd,ufd->umf/dot_general | solution.py:262
  334.3 10.4 %fusion.84 = f32[2,2048,1024]{2,1,0:T(8,128)} fusion(bf16[2,2048,512]{2,1,0:T(8,128)(2,1)} %get-tuple-element.78, bf16[2,1024,512]{2,1,0:T(8,128)(2,1)S(1)} %copy-done.31), kind=kOutput, calls=%fused_computation.166 | convolution fusion | flops 4294967296 | bytes 23068672 | tf_op jit(solution)/shard_map/umf,udf->umd/dot_general | solution.py:268
  344.7 15.4 %add_convert_fusion = bf16[2,2048,1024]{2,1,0:T(8,128)(2,1)} fusion(f32[2,2048,1024]{2,1,0:T(8,128)} %fusion.84, bf16[2,2048,512]{2,1,0:T(8,128)(2,1)} %get-tuple-element.77, bf16[2,1024,512]{2,1,0:T(8,128)(2,1)} %all-gather.15.cloned.1.call-done), kind=kOutput, calls=%fused_computation.9 | convolution fusion | flops 4303355904 | bytes 31457280 | tf_op jit(solution)/shard_map/umf,udf->umd/dot_general | solution.py:269
  369.5 14.9 %fusion.1 = (f32[2,2048]{1,0:T(2,128)S(1)}, bf16[2,2048,1024]{2,1,0:T(8,128)(2,1)}) fusion(f32[2,16,128,1024]{3,2,1,0:T(8,128)} %copy.82, f32[2,2048]{1,0:T(2,128)S(1)} %bitcast.223, bf16[2,2048,512]{2,1,0:T(8,128)(2,1)} %get-tuple-element.79, bf16[2,512,1024]{2,1,0:T(8,128)(2,1)} %all-gather.17.cloned.1.call-done), kind=kOutput, calls=%fused_computation.3 | convolution fusion | flops 4320129024 | bytes 31490048 | tf_op jit(solution)/shard_map/umf,ufd->umd/dot_general | solution.py:233
  403.1 67.2 %reduce-scatter.12.cloned.1.call-done = bf16[256,1024]{1,0:T(8,128)(2,1)} async-done(((bf16[4096,1024]{1,0:T(8,128)(2,1)}), bf16[256,1024]{1,0:T(8,128)(2,1)}) %reduce-scatter.12.cloned.1.call-update) | async-done | bytes 524304 | tf_op jit(solution)/shard_map/reduce_scatter | solution.py:277
  476.0 20.4 %all-gather.21.cloned.1.call-done = bf16[512,1024]{1,0:T(8,128)(2,1)} async-done(((bf16[256,1024]{1,0:T(8,128)(2,1)}), bf16[512,1024]{1,0:T(8,128)(2,1)}) %all-gather.21.cloned.1.call-update) | async-done | bytes 1048592 | tf_op jit(solution)/shard_map/all_gather | solution.py:294
  518.5 10.9 %convolution_convert_fusion.1 = bf16[2,512,1024]{2,1,0:T(8,128)(2,1)} fusion(bf16[2,2048,512]{2,1,0:T(8,128)(2,1)} %get-tuple-element.79, bf16[2,2048,1024]{2,1,0:T(8,128)(2,1)} %fusion.2), kind=kOutput, calls=%fused_computation.44 | convolution fusion | flops 4296015872 | bytes 14680064 | tf_op jit(solution)/shard_map/umf,umd->ufd/dot_general | solution.py:280
  529.7 10.6 %convolution_convert_fusion.3 = bf16[2,1024,512]{2,1,0:T(8,128)(2,1)} fusion(bf16[2,2048,1024]{2,1,0:T(8,128)(2,1)} %bitcast.200, bf16[2,2048,512]{2,1,0:T(8,128)(2,1)} %get-tuple-element.78), kind=kOutput, calls=%fused_computation.46 | convolution fusion | flops 4296015872 | bytes 14680064 | tf_op jit(solution)/shard_map/umd,umf->udf/dot_general | solution.py:281
  540.3 10.6 %convolution_convert_fusion.2 = bf16[2,1024,512]{2,1,0:T(8,128)(2,1)} fusion(bf16[2,2048,1024]{2,1,0:T(8,128)(2,1)} %bitcast.201, bf16[2,2048,512]{2,1,0:T(8,128)(2,1)} %get-tuple-element.77), kind=kOutput, calls=%fused_computation.45 | convolution fusion | flops 4296015872 | bytes 14680064 | tf_op jit(solution)/shard_map/umd,umf->udf/dot_general | solution.py:282
  562.3 58.2 %all-reduce.11.cloned.1.call-done = (bf16[1024,512]{1,0:T(8,128)(2,1)}, bf16[1024,256]{1,0:T(8,128)(2,1)}, bf16[1024,256]{1,0:T(8,128)(2,1)}, bf16[512,1024]{1,0:T(8,128)(2,1)}) async-done(((bf16[1024,512]{1,0:T(8,128)(2,1)}, bf16[1024,256]{1,0:T(8,128)(2,1)}, bf16[1024,256]{1,0:T(8,128)(2,1)}, bf16[512,1024]{1,0:T(8,128)(2,1)}), (bf16[1024,512]{1,0:T(8,128)(2,1)}, bf16[1024,256]{1,0:T(8,128)(2,1)}, ...) | async-done | bytes 3145744 | tf_op jit(solution)/shard_map/psum | solution.py:348
  620.9 32.8 %all-reduce.7.cloned.1.call-done = f32[1024,32]{0,1:T(8,128)} async-done(((f32[1024,32]{0,1:T(8,128)}), f32[1024,32]{0,1:T(8,128)}) %all-reduce.7.cloned.1.call-update) | async-done | bytes 131088 | tf_op jit(solution)/shard_map/psum | solution.py:357
  670.8 92.7 %reduce-scatter.10.cloned.1.call-done = bf16[256,1024]{1,0:T(8,128)(2,1)} async-done(((bf16[4096,1024]{1,0:T(8,128)(2,1)}), bf16[256,1024]{1,0:T(8,128)(2,1)}) %reduce-scatter.10.cloned.1.call-update) | async-done | bytes 524304 | tf_op jit(solution)/shard_map/reduce_scatter | solution.py:244
  772.0 32.1 %all-reduce = (f32[1024]{0:T(1024)}, f32[1024]{0:T(1024)}) all-reduce(f32[1024]{0:T(1024)S(1)} %get-tuple-element.69, f32[1024]{0:T(1024)S(1)} %get-tuple-element.70), channel_id=1, replica_groups=mesh['exp'=16,'tp'=2] {'exp'}, use_global_device_ids=true, to_apply=%region_24.25 | all-reduce | flops 2048 | bytes 16384 | tf_op jit(solution)/shard_map/psum | solution.py:356
  808.2 80.5 %all-reduce.9.cloned.1.call-done = f32[1024,32]{0,1:T(8,128)} async-done(((f32[1024,32]{0,1:T(8,128)}), f32[1024,32]{0,1:T(8,128)}) %all-reduce.9.cloned.1.call-update) | async-done | bytes 131088 | tf_op jit(solution)/shard_map/psum | solution.py:356
  (214 shorter events, 192.6 us)
Async XLA Ops:
  8.0 51.1 %copy-start = (bf16[1024,1024]{1,0:T(8,128)(2,1)S(1)}, bf16[1024,1024]{1,0:T(8,128)(2,1)}, u32[]{:S(2)}) copy-start(bf16[1024,1024]{1,0:T(8,128)(2,1)} %param.19) | copy-start | bytes 6291460
  8.0 28.2 %all-gather.9.cloned.1.call-start = ((), (), s32[]{:S(2)}) async-start(), calls=%async_computation.8 | async-start | bytes 1572864 | tf_op jit(solution)/shard_map/all_gather | solution.py:171
  12.1 81.1 %reduce-scatter.8.cloned.1.call-start = ((), (), s32[]{:S(2)}) async-start(), calls=%async_computation.9 | async-start | bytes 3145728 | tf_op jit(solution)/shard_map/reduce_scatter | solution.py:194
  61.2 78.6 %all-gather.19.cloned.1.call-start = ((), (), s32[]{:S(2)}) async-start(), calls=%async_computation.15 | async-start | bytes 8912896 | tf_op jit(solution)/shard_map/all_gather | solution.py:142
  61.8 153.7 %all-gather.11.cloned.1.call-start = ((), (), s32[]{:S(2)}) async-start(), calls=%async_computation.10 | async-start | bytes 8912896 | tf_op jit(solution)/shard_map/all_gather | solution.py:207
  95.8 152.6 %all-gather.13.cloned.1.call-start = ((), (), s32[]{:S(2)}) async-start(), calls=%async_computation.11 | async-start | bytes 3145728 | tf_op jit(solution)/shard_map/all_gather | solution.py:136
  96.4 186.6 %all-gather.15.cloned.1.call-start = ((), (), s32[]{:S(2)}) async-start(), calls=%async_computation.12 | async-start | bytes 3145728 | tf_op jit(solution)/shard_map/all_gather | solution.py:137
  97.1 220.5 %all-gather.17.cloned.1.call-start = ((), (), s32[]{:S(2)}) async-start(), calls=%async_computation.13 | async-start | bytes 3145728 | tf_op jit(solution)/shard_map/all_gather | solution.py:138
  97.8 372.4 %reduce-scatter.12.cloned.1.call-start = ((), (), s32[]{:S(2)}) async-start(), calls=%async_computation.16 | async-start | bytes 8912896 | tf_op jit(solution)/shard_map/reduce_scatter | solution.py:277
  146.8 68.7 %copy-start.13 = (bf16[1024,32]{0,1:T(8,128)(2,1)S(1)}, bf16[1024,32]{0,1:T(8,128)(2,1)}, u32[]{:S(2)}) copy-start(bf16[1024,32]{0,1:T(8,128)(2,1)} %param.21) | copy-start | bytes 196612
  388.0 12.1 %all-to-all-start = ((f32[16,2,256]{2,1,0:T(2,128)}), f32[16,2,256]{2,1,0:T(2,128)}, u32[]{:S(2)}, u32[]{:S(2)}) async-start(f32[16,2,256]{2,1,0:T(2,128)} %bitcast.225), calls=%async_computation.3 | async-start | bytes 65536 | tf_op jit(solution)/shard_map/all_to_all | solution.py:257
  393.6 102.7 %all-gather.21.cloned.1.call-start = ((), (), s32[]{:S(2)}) async-start(), calls=%async_computation.17 | async-start | bytes 1572864 | tf_op jit(solution)/shard_map/all_gather | solution.py:294
  475.2 145.3 %all-reduce.11.cloned.1.call-start = ((), (), s32[]{:S(2)}) async-start(), calls=%async_computation.25 | async-start | bytes 6291456 | tf_op jit(solution)/shard_map/psum | solution.py:348
  516.5 137.2 %all-reduce.7.cloned.1.call-start = ((), (), s32[]{:S(2)}) async-start(), calls=%async_computation.20 | async-start | bytes 262144 | tf_op jit(solution)/shard_map/psum | solution.py:357
  518.4 135.3 %reduce-scatter.20.cloned.1.call-start = ((), (), s32[]{:S(2)}) async-start(), calls=%async_computation.24 | async-start | bytes 3145728 | tf_op jit(solution)/shard_map/reduce_scatter | solution.py:343
  529.4 127.2 %reduce-scatter.16.cloned.1.call-start = ((), (), s32[]{:S(2)}) async-start(), calls=%async_computation.22 | async-start | bytes 3145728 | tf_op jit(solution)/shard_map/reduce_scatter | solution.py:337
  540.3 119.0 %reduce-scatter.18.cloned.1.call-start = ((), (), s32[]{:S(2)}) async-start(), calls=%async_computation.23 | async-start | bytes 3145728 | tf_op jit(solution)/shard_map/reduce_scatter | solution.py:340
  551.0 118.1 %reduce-scatter.14.cloned.1.call-start = ((), (), s32[]{:S(2)}) async-start(), calls=%async_computation.18 | async-start | bytes 1572864 | tf_op jit(solution)/shard_map/reduce_scatter | solution.py:325
  555.2 208.3 %reduce-scatter.10.cloned.1.call-start = ((), (), s32[]{:S(2)}) async-start(), calls=%async_computation.14 | async-start | bytes 8912896 | tf_op jit(solution)/shard_map/reduce_scatter | solution.py:244
  562.2 241.9 %all-gather.23.cloned.1.call-start = ((), (), s32[]{:S(2)}) async-start(), calls=%async_computation.19 | async-start | bytes 3145728 | tf_op jit(solution)/shard_map/all_gather | solution.py:299
  620.5 48.6 %copy-start.29 = (f32[256]{0:T(256)S(1)}, f32[256]{0:T(256)}, u32[]{:S(2)}) copy-start(f32[256]{0:T(256)} %copy-done.28) | copy-start | bytes 3076
  620.5 268.2 %all-reduce.9.cloned.1.call-start = ((), (), s32[]{:S(2)}) async-start(), calls=%async_computation.21 | async-start | bytes 262144 | tf_op jit(solution)/shard_map/psum | solution.py:356
  653.7 109.8 %copy-start.21 = (f32[1024]{0:T(1024)S(1)}, f32[1024]{0:T(1024)}, u32[]{:S(2)}) copy-start(f32[1024]{0:T(1024)} %param.20) | copy-start | bytes 12292
  653.7 109.8 %copy-start.27 = (f32[256]{0:T(256)S(1)}, f32[256]{0:T(256)}, u32[]{:S(2)}) copy-start(f32[256]{0:T(256)} %copy-done.26) | copy-start | bytes 3076
  (31 other events, 267.8 us)
Sparse Core Ops, SparseCore 0:
  12.2 23.9 all-gather.8
  61.3 31.8 reduce-scatter.7
  475.3 20.9 all-gather.20
  529.5 31.8 reduce-scatter.19
  564.1 31.8 reduce-scatter.15
  598.7 31.8 reduce-scatter.17
  633.4 20.7 reduce-scatter.13
  658.8 104.6 reduce-scatter.9
  765.1 32.8 all-gather.22
  801.7 86.9 all-reduce.8
Sparse Core Ops, SparseCore 1:
  64.1 75.6 all-gather.18
  142.6 72.8 all-gather.10
  217.0 31.3 all-gather.12
  250.0 32.9 all-gather.14
  284.6 32.9 all-gather.16
  367.0 103.2 reduce-scatter.11
  516.5 103.9 all-reduce.10
  623.3 30.3 all-reduce.6
